TPU v7x, 32 devices: a whole 2x2x4 slice. The times are simulated.
32 devices in a mesh: row: 8 (over y, x, core), col: 4 (over z).
Axes of the slice: x: 2, y: 2, z: 4, core: 2. Of those that a mesh axis runs over, the one named last changes fastest.
Arguments:
- features: bfloat16 [4096, 512], P(('row', 'col')), may hold values from -6 to 6
- coefs: bfloat16 [4096], P(('row', 'col')), may hold values from -150 to 150
Outputs:
- grads: bfloat16 [4096, 512], P(('row', 'col'))
- recolored: bfloat16 [4096, 512], P(('row', 'col'))
All inputs are finite; a program needn't handle non-finite values.
Results may differ from a plain program's by a relative error of at most 0.0025.
The roundings to bfloat16 on the way count: a program that leaves them out, or rounds other values in their place, can miss the bound.
Values may be sent and summed in bfloat16 or wider, within the bound.
A program may use at most 64 MiB of HBM per device.

v0:
```python
import jax
import jax.numpy as jnp
from jax import lax
from jax.sharding import PartitionSpec as P


def tile_terms(row_points, row_norms, col_points, col_coefs):
    width = row_points.shape[1]
    gamma = 2.0 / width
    col_full = col_points.astype(jnp.float32)
    col_norms = jnp.sum(col_full * col_full, axis=1)
    weighted = (col_coefs.astype(jnp.float32)[:, None] * col_full).astype(jnp.bfloat16)
    row_count = row_points.shape[0]
    strip_len = min(512, row_count)
    strip_count = row_count // strip_len

    def one_strip(packed):
        strip_points, strip_norms = packed
        products = lax.dot_general(
            strip_points, col_points, (((1,), (1,)), ((), ())), preferred_element_type=jnp.float32
        )
        kernel = jnp.exp(
            -(strip_norms[:, None] + col_norms[None, :] - 2.0 * products) * gamma
        ).astype(jnp.bfloat16)
        totals = jnp.dot(kernel, col_coefs, preferred_element_type=jnp.float32)
        moments = jnp.dot(kernel, weighted, preferred_element_type=jnp.float32)
        return (totals, moments)

    totals, moments = lax.map(
        one_strip,
        (
            row_points.reshape(strip_count, strip_len, width),
            row_norms.reshape(strip_count, strip_len),
        ),
    )
    return (totals.reshape(row_count), moments.reshape(row_count, width))


def local(features, coefs):
    width = features.shape[1]
    gamma = 2.0 / width
    row_points = lax.all_gather(features, "col", axis=0, tiled=True)
    row_full = row_points.astype(jnp.float32)
    row_norms = jnp.sum(row_full * row_full, axis=1)
    col_points, col_coefs = (
        lax.all_gather(features, "row", axis=0, tiled=True),
        lax.all_gather(coefs, "row", axis=0, tiled=True),
    )
    totals, moments = tile_terms(row_points, row_norms, col_points, col_coefs)
    own_totals, own_moments = (
        lax.psum_scatter(totals, "col", scatter_dimension=0, tiled=True),
        lax.psum_scatter(moments, "col", scatter_dimension=0, tiled=True),
    )
    own_full = features.astype(jnp.float32)
    grads = (2.0 * gamma * (own_moments - own_totals[:, None] * own_full)).astype(jnp.bfloat16)
    gram = jnp.einsum("pa,pb->ab", grads, grads, preferred_element_type=jnp.float32)
    point_count = features.shape[0] * lax.axis_size("row") * lax.axis_size("col")
    whole_gram = lax.psum(gram, ("row", "col"))
    agop = (whole_gram / point_count).astype(jnp.bfloat16)
    recolored = jnp.dot(features, agop, preferred_element_type=jnp.float32)
    return (grads, recolored.astype(jnp.bfloat16))


def solution(mesh):
    return jax.shard_map(
        local,
        mesh=mesh,
        in_specs=(P(("row", "col"), None), P(("row", "col"))),
        out_specs=(P(("row", "col"), None), P(("row", "col"), None)),
        check_vma=False,
    )
```

profile of v0, /device:TPU:0, one launch (start us, length us, event | category | flops | bytes accessed | tf_op | source)
XLA Modules:
  0.0 211.3 jit_solution(17170503718108234027)
XLA Ops:
  7.2 0.0 all-gather.3.cloned.1.call-start
  7.2 0.7 all-gather.3.cloned.1.call-update
  7.9 0.0 reduce-scatter.2.cloned.1.call-start
  7.9 10.3 %all-gather = bf16[8,1,128]{2,1,0:T(2,128)(2,1)S(1)} all-gather(bf16[1,1,128]{2,1,0:T(2,128)(2,1)} %bitcast.18), channel_id=1, replica_groups=mesh['row'=8,'col'=4] {'row'}, dimensions={0}, use_global_device_ids=true | all-gather | bytes 2304 | tf_op jit(solution)/shard_map/all_gather | solution.py:47
  18.3 16.5 %all_gather.9 = bf16[512,512]{1,0:T(8,128)(2,1)S(1)} all-gather(bf16[128,512]{1,0:T(8,128)(2,1)} %param.2), channel_id=1, replica_groups=mesh['row'=8,'col'=4] {'col'}, dimensions={0}, use_global_device_ids=true | all-gather | bytes 655360 | tf_op jit(solution)/shard_map/all_gather | solution.py:42
  34.8 0.2 multiply_reduce_fusion
  35.0 1.1 all-gather.3.cloned.1.call-done
  36.1 1.6 fusion
  37.7 0.8 exponential_convert_fusion
  38.6 1.8 fusion.3
  40.4 0.0 reduce-scatter.2.cloned.1.call-update
  40.4 0.0 all-reduce.3.cloned.1.call-start
  40.4 0.6 copy-done.3
  41.0 0.6 dynamic-slice.2
  42.2 0.4 fusion.7
  42.6 11.9 %all-reduce = f32[512]{0:T(512)S(1)} all-reduce(f32[512]{0:T(512)S(1)} %bitcast.17), channel_id=3, replica_groups=mesh['row'=8,'col'=4] {'col'}, use_global_device_ids=true, to_apply=%region_3.4.clone | all-reduce | flops 512 | bytes 4096
  54.5 0.1 dynamic-slice.3
  54.6 13.2 %reduce-scatter.2.cloned.1.call-done = f32[128,512]{1,0:T(8,128)} async-done(((f32[512,512]{1,0:T(8,128)}), f32[128,512]{1,0:T(8,128)}) %reduce-scatter.2.cloned.1.call-update) | async-done | bytes 262160 | tf_op jit(solution)/shard_map/reduce_scatter | solution.py:52
  67.8 1.1 multiply_convert_fusion.2
  68.8 1.4 fusion.10
  70.2 0.0 all-reduce.3.cloned.1.call-update
  70.2 132.2 %all-reduce.3.cloned.1.call-done = f32[512,512]{1,0:T(8,128)} async-done(((f32[512,512]{1,0:T(8,128)}), f32[512,512]{1,0:T(8,128)}) %all-reduce.3.cloned.1.call-update) | async-done | bytes 1048592 | tf_op jit(solution)/shard_map/psum | solution.py:58
  202.4 1.6 fusion.2
  204.0 0.8 copy.6
  (9 shorter events, 0.0 us)
Async XLA Ops:
  7.2 28.9 %all-gather.3.cloned.1.call-start = ((), (), s32[]{:S(2)}) async-start(), calls=%async_computation.1 | async-start | bytes 1179648 | tf_op jit(solution)/shard_map/all_gather | solution.py:46
  7.9 59.9 %reduce-scatter.2.cloned.1.call-start = ((), (), s32[]{:S(2)}) async-start(), calls=%async_computation.2 | async-start | bytes 1310720 | tf_op jit(solution)/shard_map/reduce_scatter | solution.py:52
  36.1 1.6 copy-start.2
  40.4 0.7 copy-start.3
  40.4 27.4 %copy-start = (bf16[128,512]{1,0:T(8,128)(2,1)S(1)}, bf16[128,512]{1,0:T(8,128)(2,1)}, u32[]{:S(2)}) copy-start(bf16[128,512]{1,0:T(8,128)(2,1)} %param.2) | copy-start | bytes 393220
  40.4 162.0 %all-reduce.3.cloned.1.call-start = ((), (), s32[]{:S(2)}) async-start(), calls=%async_computation.3 | async-start | bytes 2097152 | tf_op jit(solution)/shard_map/psum | solution.py:58
  68.8 1.4 copy-start.1
Sparse Core Ops, SparseCore 0:
  9.9 26.1 all-gather.2
  40.5 27.2 reduce-scatter.1
  73.8 128.5 all-reduce.2
where the time goes:
time: 212 us; the launch traced here: 211 us
  waiting for transfers between devices  147 us (69%)
  blocking collectives  38.7 us (18%)
  between operations  14.5 us (7%)
  matrix products  5.93 us (3%)
  other arithmetic  2.84 us (1%)
    psum x1, waiting for transfers between devices, local(): whole_gram = lax.psum(gram, ('row', 'col'))  132 us
    all_gather x1, blocking collectives, local(): row_points = lax.all_gather(features, 'col', axis=0, tiled=True)  16.5 us
    reduce_scatter x1, waiting for transfers between devices, local(): lax.psum_scatter(moments, 'col', scatter_dimension=0, tiled=True)  13.2 us
    unnamed x1, blocking collectives  11.9 us
    all_gather x1, blocking collectives, local(): lax.all_gather(coefs, 'row', axis=0, tiled=True)  10.3 us
  transfers between devices with their start and end apart: 3, of which 3 were waited for; matrix products, arithmetic and copies ran while one was open for 1% of the time, Pallas kernels for 0%

commit v1 on v0

v1 whole, which is shorter than its diff:
```python
import functools

import jax
import jax.numpy as jnp
from jax import lax
from jax.experimental import pallas as pl
from jax.experimental.pallas import tpu as pltpu
from jax.sharding import PartitionSpec as P

MESH = pl.DeviceIdType.MESH
NT = (((1,), (1,)), ((), ()))
TN = (((0,), (0,)), ((), ()))


def flipped(value, bits):
    bit = 1
    while bit <= bits:
        if bits & bit:
            value = value + bit - 2 * bit * lax.rem(lax.div(value, bit), 2)
        bit *= 2
    return value


def kernel(
    planes, cols, point_count,
    feat_ref, coef_ref, grads_ref, rec_ref,
    rows, buf, info, norms, mom, tot, part, part_in, whole_grads,
    gram, gram_out, gram_in, agop, rec_out, rec_in,
    sib_s, sib_r, info_s, info_r, blk_s, blk_r, diag_s, diag_r,
    part_s, part_r, gram_s, gram_r, agop_s, agop_r, rec_s, rec_r,
):
    count, width = feat_ref.shape
    gamma = 2.0 / width
    half = width // 2
    chips = planes * cols
    row = lax.axis_index("row")
    z = lax.axis_index("col")
    p, core = lax.div(row, 2), lax.rem(row, 2)
    peers = [(d, k) for k in range(cols) for d in range(planes) if (d, k) != (0, 0)]

    def chip(d, k):
        return (flipped(p, d) * 2 + core, flipped(z, k))

    sibling = (flipped(row, 1), z)

    def copy(src, dst, send, recv, device):
        return pltpu.make_async_remote_copy(
            src_ref=src, dst_ref=dst, send_sem=send, recv_sem=recv,
            device_id=device, device_id_type=MESH,
        )

    barrier = pltpu.get_barrier_semaphore()
    pl.semaphore_signal(barrier, inc=1, device_id=sibling, device_id_type=MESH)
    for d, k in peers:
        pl.semaphore_signal(barrier, inc=1, device_id=chip(d, k), device_id_type=MESH)

    own_full = feat_ref[...].astype(jnp.float32)
    own_norms = jnp.sum(own_full * own_full, axis=1, keepdims=True)
    info[0, 0, 0:1, :] = coef_ref[...]
    info[0, 0, 1:2, :] = jnp.transpose(jnp.broadcast_to(own_norms, (count, 128)))[0:1, :]
    info[0, 0, 2:8, :] = jnp.zeros((6, count), jnp.float32)
    rows[pl.ds(core, 1)] = feat_ref[...][None]
    mom[...] = jnp.zeros_like(mom)
    tot[...] = jnp.zeros_like(tot)
    pl.semaphore_wait(barrier, chips)

    sent = []

    def send(*args):
        made = copy(*args)
        made.start()
        sent.append(made)
        return made

    from_sib = send(feat_ref, rows.at[core], sib_s, sib_r, sibling)
    blocks, diagonals, infos = {}, {}, {}
    relay = planes == 4

    def spread(k):
        for e in ((1, 2) if relay else range(1, planes)):
            source = feat_ref if k == 0 else buf.at[0, k]
            blocks[e, k] = send(source, buf.at[e, k], blk_s.at[e, k], blk_r.at[e, k], chip(e, 0))

    def forward(k):
        upper, lower = pl.ds(0, count // 2), pl.ds(count // 2, count // 2)
        blocks[1, k].wait_recv()
        blocks[3, k] = send(
            buf.at[1, k, upper], buf.at[3, k, upper], blk_s.at[3, k], blk_r.at[3, k], chip(2, 0)
        )
        blocks[2, k].wait_recv()
        diagonals[k] = send(
            buf.at[2, k, lower], buf.at[3, k, lower], diag_s.at[k], diag_r.at[k], chip(1, 0)
        )

    for k in range(1, cols):
        blocks[0, k] = send(feat_ref, buf.at[0, k], blk_s.at[0, k], blk_r.at[0, k], chip(0, k))
    spread(0)
    for d, k in peers:
        infos[d, k] = send(
            info.at[0, 0], info.at[d, k], info_s.at[d, k], info_r.at[d, k], chip(d, k)
        )

    from_sib.wait_recv()
    both = rows[...].reshape(2 * count, width)
    both_full = both.astype(jnp.float32)
    norms[...] = jnp.sum(both_full * both_full, axis=1, keepdims=True)

    def add_block(points, facts):
        coefs = facts[0:1, :]
        col_norms = facts[1:2, :]
        products = lax.dot_general(
            rows[...].reshape(2 * count, width), points, NT, preferred_element_type=jnp.float32
        )
        kern = jnp.exp(-(norms[...] + col_norms - 2.0 * products) * gamma).astype(jnp.bfloat16)
        tall = jnp.transpose(jnp.broadcast_to(coefs, (128, count)))[:, 0:1]
        weighted = (tall * points.astype(jnp.float32)).astype(jnp.bfloat16)
        tot[...] += kern.astype(jnp.float32) * coefs
        mom[...] += jnp.dot(kern, weighted, preferred_element_type=jnp.float32)

    add_block(feat_ref[...], info[0, 0])
    if relay:
        def take(d, k):
            infos[d, k].wait_recv()
            if d == 3:
                blocks[d, k].wait_recv()
                diagonals[k].wait_recv()
            add_block(buf[d, k], info[d, k])

        for k in range(1, cols + 1):
            if k < cols:
                blocks[0, k].wait_recv()
                spread(k)
            forward(k - 1)
            if k < cols:
                take(0, k)
            take(1, k - 1)
            take(2, k - 1)
            if k > 1:
                take(3, k - 2)
        take(3, cols - 1)
    else:
        for k in range(1, cols):
            blocks[0, k].wait_recv()
            spread(k)
        for d, k in peers:
            infos[d, k].wait_recv()
            if d:
                blocks[d, k].wait_recv()

        @pl.loop(1, chips)
        def _(at):
            d, k = lax.div(at, cols), lax.rem(at, cols)
            add_block(buf[d, k], info[d, k])

    totals = jnp.sum(tot[...], axis=1, keepdims=True)
    part[...] = mom[...] - totals * rows[...].reshape(2 * count, width).astype(jnp.float32)
    send(part, part_in, part_s, part_r, sibling).wait_recv()
    both_grads = (2.0 * gamma * (part[...] + part_in[...])).astype(jnp.bfloat16)
    whole_grads[...] = both_grads
    grads_ref[...] = whole_grads[pl.ds(pl.multiple_of(core * count, count), count), :]

    owners, depth = gram.shape[0], gram.shape[1]
    mine = pl.ds(pl.multiple_of(core * half, half), half)
    product = lax.dot_general(
        whole_grads[:, mine], whole_grads[...], TN, preferred_element_type=jnp.float32
    )
    gram[...] = product.reshape(owners, depth, width)
    gram_out[...] = product.astype(jnp.bfloat16).reshape(owners, depth, width)

    me = p * cols + z
    every = owners == chips

    def owning(index, do):
        if every:
            do()
        else:
            pl.when(index < owners)(do)

    def place(index):
        return index if every else lax.rem(index, owners)

    def gram_copy(d, k):
        return copy(
            gram_out.at[place(flipped(p, d) * cols + flipped(z, k))], gram_in.at[d, k],
            gram_s.at[d, k], gram_r.at[d, k], chip(d, k),
        )

    def agop_copy(d, k):
        at = agop.at[place(me)]
        return copy(at, at, agop_s.at[d, k], agop_r.at[d, k], chip(d, k))

    for d, k in peers:
        owning(flipped(p, d) * cols + flipped(z, k), gram_copy(d, k).start)

    def reduce_own():
        total = gram[place(me)]
        for d, k in peers:
            gram_copy(d, k).wait_recv()
            total += gram_in[d, k].astype(jnp.float32)
        agop[place(me)] = (total / point_count).astype(jnp.bfloat16)
        for d, k in peers:
            agop_copy(d, k).start()

    owning(me, reduce_own)
    for d, k in peers:
        owning(flipped(p, d) * cols + flipped(z, k), agop_copy(d, k).wait_recv)

    colored = lax.dot_general(
        rows[...].reshape(2 * count, width), agop[...].reshape(half, width), NT,
        preferred_element_type=jnp.float32,
    ).astype(jnp.bfloat16).reshape(2, count, half)
    rec_out[...] = colored
    swap = send(rec_out.at[1 - core], rec_in, rec_s, rec_r, sibling)
    rec_ref[:, mine] = rec_out[core]
    swap.wait_recv()
    rec_ref[:, pl.ds(pl.multiple_of((1 - core) * half, half), half)] = rec_in[...]

    for made in sent:
        made.wait_send()
    for d, k in peers:
        owning(flipped(p, d) * cols + flipped(z, k), gram_copy(d, k).wait_send)

    def agop_sent():
        for d, k in peers:
            agop_copy(d, k).wait_send()

    owning(me, agop_sent)


def local(planes, cols, features, coefs):
    count, width = features.shape
    chips = planes * cols
    half = width // 2
    owners = min(chips, half // 16)
    depth = half // owners
    bf16, f32 = jnp.bfloat16, jnp.float32
    dma = pltpu.SemaphoreType.DMA
    vmem = pltpu.VMEM
    return pl.pallas_call(
        functools.partial(kernel, planes, cols, count * chips * 2),
        out_shape=[jax.ShapeDtypeStruct((count, width), bf16)] * 2,
        in_specs=[pl.BlockSpec(memory_space=vmem)] * 2,
        out_specs=[pl.BlockSpec(memory_space=vmem)] * 2,
        scratch_shapes=[
            vmem((2, count, width), bf16),
            vmem((planes, cols, count, width), bf16),
            vmem((planes, cols, 8, count), f32),
            vmem((2 * count, 1), f32),
            vmem((2 * count, width), f32),
            vmem((2 * count, count), f32),
            vmem((2 * count, width), f32),
            vmem((2 * count, width), f32),
            vmem((2 * count, width), bf16),
            vmem((owners, depth, width), f32),
            vmem((owners, depth, width), bf16),
            vmem((planes, cols, depth, width), bf16),
            vmem((owners, depth, width), bf16),
            vmem((2, count, half), bf16),
            vmem((count, half), bf16),
            dma(()), dma(()),
            dma((planes, cols)), dma((planes, cols)),
            dma((planes, cols)), dma((planes, cols)),
            dma((cols,)), dma((cols,)),
            dma(()), dma(()),
            dma((planes, cols)), dma((planes, cols)),
            dma((planes, cols)), dma((planes, cols)),
            dma(()), dma(()),
        ],
        compiler_params=pltpu.CompilerParams(
            collective_id=0, has_side_effects=True, vmem_limit_bytes=40 * 1024 * 1024
        ),
        cost_estimate=pl.CostEstimate(
            flops=8 * count * count * chips * width,
            bytes_accessed=6 * count * width,
            transcendentals=2 * count * count * chips,
        ),
    )(features, coefs.astype(f32).reshape(1, count))


def solution(mesh):
    return jax.shard_map(
        functools.partial(local, mesh.shape["row"] // 2, mesh.shape["col"]),
        mesh=mesh,
        in_specs=(P(("row", "col"), None), P(("row", "col"))),
        out_specs=(P(("row", "col"), None), P(("row", "col"), None)),
        check_vma=False,
    )
```

time: 212 us -> 53.8 us (0.25)
  waiting for transfers between devices: 147 us -> 0 us
  Pallas kernels: 0 us -> 50.1 us
  blocking collectives: 38.7 us -> 0 us
  between operations: 14.5 us -> 0.64 us
  matrix products: 5.93 us -> 0 us
  other arithmetic: 2.84 us -> 0.66 us
    psum x1 -> x0, waiting for transfers between devices: 132 us -> none  [local(): whole_gram = lax.psum(gram, ('row', 'col'))]
    pallas_call x0 -> x1, Pallas kernels: none -> 50.1 us  [local(): pl.pallas_call(functools.partial(kernel, planes, cols, count * chips * 2)...]
    all_gather x2 -> x0, blocking collectives: 26.8 us -> none  [the longest x1 16.5 us: local(): row_points = lax.all_gather(features, 'col', axis=0, tiled=True)]
    reduce_scatter x1 -> x0, waiting for transfers between devices: 13.2 us -> none  [local(): lax.psum_scatter(moments, 'col', scatter_dimension=0, tiled=True)]
    unnamed x1 -> x0, blocking collectives: 11.9 us -> none
    dot_general x5 -> x0, matrix products: 5.93 us -> none  [the longest x1 1.79 us: one_strip(): moments = jnp.dot(kernel, weighted, preferred_element_type=jnp.float32)]
  transfers between devices with their start and end apart: 3 -> 0, of which waited for: 3 -> 0; matrix products, arithmetic and copies ran while one was open for 1% -> 0% of each run, Pallas kernels for 0% -> 0%
where the time goes in v1:
time: 53.8 us; the launch traced here: 53.6 us
  Pallas kernels  50.1 us (93%)
  local copies, waits for them, and re-layouts  2.22 us (4%)
  other arithmetic  0.66 us (1%)
  between operations  0.64 us (1%)
    pallas_call x1, Pallas kernels, local(): pl.pallas_call(functools.partial(kernel, planes, cols, count * chips * 2)...  50.1 us
    unnamed x4, local copies, waits for them, and re-layouts  2.22 us

profile of v1, /device:TPU:0, one launch (start us, length us, event | category | flops | bytes accessed | tf_op | source)
XLA Modules:
  0.0 53.6 jit_solution(15759746677869132840)
XLA Ops:
  0.6 0.7 %bitcast_convert_fusion.coef_ref = f32[1,128]{1,0:T(1,128)S(1)} fusion(bf16[128]{0:T(256)(128)(2,1)} %param.3), kind=kLoop, calls=%fused_computation | loop fusion | flops 128 | bytes 768 | tf_op jit(solution)/shard_map/reshape | solution.py:277
  1.3 0.0 copy-start
  1.3 0.9 %copy-done = bf16[128,512]{1,0:T(8,128)(2,1)S(1)} copy-done((bf16[128,512]{1,0:T(8,128)(2,1)S(1)}, bf16[128,512]{1,0:T(8,128)(2,1)}, u32[]{:S(2)}) %copy-start) | copy-done | bytes 131096
  2.2 50.1 %shard_map.41 = (bf16[128,512]{1,0:T(8,128)(2,1)S(1)}, bf16[128,512]{1,0:T(8,128)(2,1)S(1)}) custom-call(bf16[128,512]{1,0:T(8,128)(2,1)S(1)} %copy-done, f32[1,128]{1,0:T(1,128)S(1)} %bitcast_convert_fusion.coef_ref), custom_call_target="tpu_custom_call" | custom-call | flops 1073741824 | bytes 393216 | tf_op jit(solution)/shard_map/pallas_call | solution.py:239
  52.3 0.7 %copy.6 = bf16[128,512]{1,0:T(8,128)(2,1)} copy(bf16[128,512]{1,0:T(8,128)(2,1)S(1)} %get-tuple-element.4) | data formatting | bytes 262144
  53.0 0.7 %copy.7 = bf16[128,512]{1,0:T(8,128)(2,1)} copy(bf16[128,512]{1,0:T(8,128)(2,1)S(1)} %get-tuple-element.5) | data formatting | bytes 262144
Async XLA Ops:
  1.3 0.9 %copy-start = (bf16[128,512]{1,0:T(8,128)(2,1)S(1)}, bf16[128,512]{1,0:T(8,128)(2,1)}, u32[]{:S(2)}) copy-start(bf16[128,512]{1,0:T(8,128)(2,1)} %feat_ref.1) | copy-start | bytes 393220

commit v2 on v1

--- a/solution.py
+++ b/solution.py
@@ -21,14 +21,34 @@
     return value
 
 
+def slot_of(z, block, cols):
+    far = jnp.abs(block - z)
+    both = jnp.minimum(z, cols - 1 - z)
+    left = (block < z).astype(jnp.int32)
+    return jnp.where(far <= both, 2 * far - left, far + both)
+
+
+def arrival(z, slot, cols):
+    both = jnp.minimum(z, cols - 1 - z)
+    paired = slot <= 2 * both
+    far = jnp.where(paired, (slot + 1) // 2, slot - both)
+    left = jnp.where(paired, slot % 2, (2 * z >= cols).astype(jnp.int32))
+    return z + far - 2 * far * left, left
+
+
 def kernel(
     planes, cols, point_count,
-    feat_ref, coef_ref, grads_ref, rec_ref,
+    feat_hbm, coef_hbm, grads_ref, rec_ref,
+    feat_ref, coef_ref, in_s,
     rows, buf, info, norms, mom, tot, part, part_in, whole_grads,
     gram, gram_out, gram_in, agop, rec_out, rec_in,
-    sib_s, sib_r, info_s, info_r, blk_s, blk_r, diag_s, diag_r,
+    line_s, sib_s, sib_r, info_s, info_r, blk_s, blk_r, diag_s, diag_r,
     part_s, part_r, gram_s, gram_r, agop_s, agop_r, rec_s, rec_r,
 ):
+    load_feats = pltpu.make_async_copy(feat_hbm, feat_ref, in_s.at[0])
+    load_coefs = pltpu.make_async_copy(coef_hbm, coef_ref, in_s.at[1])
+    load_feats.start()
+    load_coefs.start()
     count, width = feat_ref.shape
     gamma = 2.0 / width
     half = width // 2
@@ -50,19 +70,29 @@
         )
 
     barrier = pltpu.get_barrier_semaphore()
-    pl.semaphore_signal(barrier, inc=1, device_id=sibling, device_id_type=MESH)
-    for d, k in peers:
-        pl.semaphore_signal(barrier, inc=1, device_id=chip(d, k), device_id_type=MESH)
-
+    relay = planes == 4
+    beside = (1, 2) if relay else range(1, planes)
+
+    def greet(device):
+        pl.semaphore_signal(barrier, inc=1, device_id=device, device_id_type=MESH)
+
+    greet(sibling)
+    for e in beside:
+        greet(chip(e, 0))
+    pl.when(z > 0)(lambda: greet((row, z - 1)))
+    pl.when(z < cols - 1)(lambda: greet((row, z + 1)))
+
+    load_feats.wait()
+    load_coefs.wait()
     own_full = feat_ref[...].astype(jnp.float32)
     own_norms = jnp.sum(own_full * own_full, axis=1, keepdims=True)
-    info[0, 0, 0:1, :] = coef_ref[...]
+    info[0, 0, 0:1, :] = coef_ref[...].astype(jnp.float32)
     info[0, 0, 1:2, :] = jnp.transpose(jnp.broadcast_to(own_norms, (count, 128)))[0:1, :]
-    info[0, 0, 2:8, :] = jnp.zeros((6, count), jnp.float32)
     rows[pl.ds(core, 1)] = feat_ref[...][None]
     mom[...] = jnp.zeros_like(mom)
     tot[...] = jnp.zeros_like(tot)
-    pl.semaphore_wait(barrier, chips)
+    on_line = (z > 0).astype(jnp.int32) + (z < cols - 1).astype(jnp.int32)
+    pl.semaphore_wait(barrier, 1 + len(beside) + on_line)
 
     sent = []
 
@@ -74,15 +104,21 @@
 
     from_sib = send(feat_ref, rows.at[core], sib_s, sib_r, sibling)
     blocks, diagonals, infos = {}, {}, {}
-    relay = planes == 4
 
     def spread(k):
-        for e in ((1, 2) if relay else range(1, planes)):
+        for e in beside:
+            infos[e, k] = send(
+                info.at[0, k], info.at[e, k], info_s.at[e, k], info_r.at[e, k], chip(e, 0)
+            )
             source = feat_ref if k == 0 else buf.at[0, k]
             blocks[e, k] = send(source, buf.at[e, k], blk_s.at[e, k], blk_r.at[e, k], chip(e, 0))
 
     def forward(k):
         upper, lower = pl.ds(0, count // 2), pl.ds(count // 2, count // 2)
+        infos[1, k].wait_recv()
+        infos[3, k] = send(
+            info.at[1, k], info.at[3, k], info_s.at[3, k], info_r.at[3, k], chip(2, 0)
+        )
         blocks[1, k].wait_recv()
         blocks[3, k] = send(
             buf.at[1, k, upper], buf.at[3, k, upper], blk_s.at[3, k], blk_r.at[3, k], chip(2, 0)
@@ -92,13 +128,40 @@
             buf.at[2, k, lower], buf.at[3, k, lower], diag_s.at[k], diag_r.at[k], chip(1, 0)
         )
 
-    for k in range(1, cols):
-        blocks[0, k] = send(feat_ref, buf.at[0, k], blk_s.at[0, k], blk_r.at[0, k], chip(0, k))
+    def along(k, block, to, sem):
+        slot = slot_of(to, block, cols)
+        facts = copy(info.at[0, k], info.at[0, slot], sem(1), info_r.at[0, slot], (row, to))
+        source = feat_ref if k == 0 else buf.at[0, k]
+        return facts, copy(source, buf.at[0, slot], sem(0), blk_r.at[0, slot], (row, to))
+
+    def line(do):
+        def to_right():
+            for made in along(0, z, z + 1, lambda at: line_s.at[0, at]):
+                do(made)
+
+        def to_left():
+            for made in along(0, z, z - 1, lambda at: line_s.at[1, at]):
+                do(made)
+
+        pl.when(z < cols - 1)(to_right)
+        pl.when(z > 0)(to_left)
+
+    def onward(k, do):
+        block, left = arrival(z, k, cols)
+        to = z - 1 + 2 * left
+
+        def both():
+            for made in along(k, block, to, lambda at: (info_s if at else blk_s).at[0, k]):
+                do(made)
+
+        pl.when(jnp.logical_and(to >= 0, to < cols))(both)
+
+    def arrived(k):
+        copy(info.at[0, 0], info.at[0, k], info_s.at[0, k], info_r.at[0, k], sibling).wait_recv()
+        copy(feat_ref, buf.at[0, k], blk_s.at[0, k], blk_r.at[0, k], sibling).wait_recv()
+
+    line(lambda made: made.start())
     spread(0)
-    for d, k in peers:
-        infos[d, k] = send(
-            info.at[0, 0], info.at[d, k], info_s.at[d, k], info_r.at[d, k], chip(d, k)
-        )
 
     from_sib.wait_recv()
     both = rows[...].reshape(2 * count, width)
@@ -120,7 +183,8 @@
     add_block(feat_ref[...], info[0, 0])
     if relay:
         def take(d, k):
-            infos[d, k].wait_recv()
+            if d > 1:
+                infos[d, k].wait_recv()
             if d == 3:
                 blocks[d, k].wait_recv()
                 diagonals[k].wait_recv()
@@ -128,7 +192,8 @@
 
         for k in range(1, cols + 1):
             if k < cols:
-                blocks[0, k].wait_recv()
+                arrived(k)
+                onward(k, lambda made: made.start())
                 spread(k)
             forward(k - 1)
             if k < cols:
@@ -140,11 +205,12 @@
         take(3, cols - 1)
     else:
         for k in range(1, cols):
-            blocks[0, k].wait_recv()
+            arrived(k)
+            onward(k, lambda made: made.start())
             spread(k)
         for d, k in peers:
-            infos[d, k].wait_recv()
             if d:
+                infos[d, k].wait_recv()
                 blocks[d, k].wait_recv()
 
         @pl.loop(1, chips)
@@ -217,6 +283,9 @@
 
     for made in sent:
         made.wait_send()
+    line(lambda made: made.wait_send())
+    for k in range(1, cols):
+        onward(k, lambda made: made.wait_send())
     for d, k in peers:
         owning(flipped(p, d) * cols + flipped(z, k), gram_copy(d, k).wait_send)
 
@@ -239,12 +308,15 @@
     return pl.pallas_call(
         functools.partial(kernel, planes, cols, count * chips * 2),
         out_shape=[jax.ShapeDtypeStruct((count, width), bf16)] * 2,
-        in_specs=[pl.BlockSpec(memory_space=vmem)] * 2,
+        in_specs=[pl.BlockSpec(memory_space=pl.ANY)] * 2,
         out_specs=[pl.BlockSpec(memory_space=vmem)] * 2,
         scratch_shapes=[
+            vmem((count, width), bf16),
+            vmem((1, count), bf16),
+            dma((2,)),
             vmem((2, count, width), bf16),
             vmem((planes, cols, count, width), bf16),
-            vmem((planes, cols, 8, count), f32),
+            vmem((planes, cols, 2, count), f32),
             vmem((2 * count, 1), f32),
             vmem((2 * count, width), f32),
             vmem((2 * count, count), f32),
@@ -257,6 +329,7 @@
             vmem((owners, depth, width), bf16),
             vmem((2, count, half), bf16),
             vmem((count, half), bf16),
+            dma((2, 2)),
             dma(()), dma(()),
             dma((planes, cols)), dma((planes, cols)),
             dma((planes, cols)), dma((planes, cols)),
@@ -274,7 +347,7 @@
             bytes_accessed=6 * count * width,
             transcendentals=2 * count * count * chips,
         ),
-    )(features, coefs.astype(f32).reshape(1, count))
+    )(features, coefs.reshape(1, count))
 
 
 def solution(mesh):

time: 53.8 us -> 49.8 us (0.926)
  Pallas kernels: 50.1 us -> 46.1 us
  other arithmetic: 0.66 us -> 0 us
  local copies, waits for them, and re-layouts: 2.22 us -> 2.86 us
    pallas_call x1, Pallas kernels: 50.1 us -> 46.1 us  [local(): pl.pallas_call(functools.partial(kernel, planes, cols, count * chips * 2)...]
    reshape x1 -> x0, other arithmetic: 0.66 us -> none  [local(): coefs.astype(f32).reshape(1, count)]
    unnamed x4 -> x6, local copies, waits for them, and re-layouts: 2.22 us -> 2.86 us
where the time goes in v2:
time: 49.8 us; the launch traced here: 49.6 us
  Pallas kernels  46.1 us (93%)
  local copies, waits for them, and re-layouts  2.86 us (6%)
  between operations  0.65 us (1%)
    pallas_call x1, Pallas kernels, local(): pl.pallas_call(functools.partial(kernel, planes, cols, count * chips * 2)...  46.1 us
    unnamed x6, local copies, waits for them, and re-layouts  2.86 us

profile of v2, /device:TPU:0, one launch (start us, length us, event | category | flops | bytes accessed | tf_op | source)
XLA Modules:
  0.0 49.6 jit_solution(14582023931480226348)
XLA Ops:
  0.6 0.0 copy-start.1
  0.6 0.6 %copy-done.1 = bf16[128]{0:T(256)(128)(2,1)S(1)} copy-done((bf16[128]{0:T(256)(128)(2,1)S(1)}, bf16[128]{0:T(256)(128)(2,1)}, u32[]{:S(2)}) %copy-start.1) | copy-done | bytes 280
  1.3 0.0 copy-start
  1.3 0.9 %copy-done = bf16[128,512]{1,0:T(8,128)(2,1)S(1)} copy-done((bf16[128,512]{1,0:T(8,128)(2,1)S(1)}, bf16[128,512]{1,0:T(8,128)(2,1)}, u32[]{:S(2)}) %copy-start) | copy-done | bytes 131096
  2.2 46.1 %shard_map.41 = (bf16[128,512]{1,0:T(8,128)(2,1)S(1)}, bf16[128,512]{1,0:T(8,128)(2,1)S(1)}) custom-call(bf16[128,512]{1,0:T(8,128)(2,1)S(1)} %copy-done, bf16[1,128]{1,0:T(2,128)(2,1)S(1)} %bitcast.1), custom_call_target="tpu_custom_call" | custom-call | flops 1073741824 | bytes 393216 | tf_op jit(solution)/shard_map/pallas_call | solution.py:308
  48.3 0.7 %copy.6 = bf16[128,512]{1,0:T(8,128)(2,1)} copy(bf16[128,512]{1,0:T(8,128)(2,1)S(1)} %get-tuple-element.4) | data formatting | bytes 262144
  49.0 0.7 %copy.7 = bf16[128,512]{1,0:T(8,128)(2,1)} copy(bf16[128,512]{1,0:T(8,128)(2,1)S(1)} %get-tuple-element.5) | data formatting | bytes 262144
Async XLA Ops:
  0.6 0.7 %copy-start.1 = (bf16[128]{0:T(256)(128)(2,1)S(1)}, bf16[128]{0:T(256)(128)(2,1)}, u32[]{:S(2)}) copy-start(bf16[128]{0:T(256)(128)(2,1)} %param.3) | copy-start | bytes 772
  1.3 0.9 %copy-start = (bf16[128,512]{1,0:T(8,128)(2,1)S(1)}, bf16[128,512]{1,0:T(8,128)(2,1)}, u32[]{:S(2)}) copy-start(bf16[128,512]{1,0:T(8,128)(2,1)} %feat_hbm.1) | copy-start | bytes 393220

commit v3 on v2

--- a/solution.py
+++ b/solution.py
@@ -41,7 +41,7 @@
     feat_hbm, coef_hbm, grads_ref, rec_ref,
     feat_ref, coef_ref, in_s,
     rows, buf, info, norms, mom, tot, part, part_in, whole_grads,
-    gram, gram_out, gram_in, agop, rec_out, rec_in,
+    gram, gram_in, agop, rec_out, rec_in,
     line_s, sib_s, sib_r, info_s, info_r, blk_s, blk_r, diag_s, diag_r,
     part_s, part_r, gram_s, gram_r, agop_s, agop_r, rec_s, rec_r,
 ):
@@ -231,7 +231,6 @@
         whole_grads[:, mine], whole_grads[...], TN, preferred_element_type=jnp.float32
     )
     gram[...] = product.reshape(owners, depth, width)
-    gram_out[...] = product.astype(jnp.bfloat16).reshape(owners, depth, width)
 
     me = p * cols + z
     every = owners == chips
@@ -247,7 +246,7 @@
 
     def gram_copy(d, k):
         return copy(
-            gram_out.at[place(flipped(p, d) * cols + flipped(z, k))], gram_in.at[d, k],
+            gram.at[place(flipped(p, d) * cols + flipped(z, k))], gram_in.at[d, k],
             gram_s.at[d, k], gram_r.at[d, k], chip(d, k),
         )
 
@@ -255,21 +254,57 @@
         at = agop.at[place(me)]
         return copy(at, at, agop_s.at[d, k], agop_r.at[d, k], chip(d, k))
 
-    for d, k in peers:
-        owning(flipped(p, d) * cols + flipped(z, k), gram_copy(d, k).start)
-
-    def reduce_own():
-        total = gram[place(me)]
+    def strip(d):
+        return pl.ds(flipped(p, d) * cols, cols)
+
+    if every:
+        planar = [
+            send(gram.at[strip(e)], gram_in.at[e], gram_s.at[e, 0], gram_r.at[e, 0], chip(e, 0))
+            for e in range(1, planes)
+        ]
+        for e, made in enumerate(planar, 1):
+            made.wait_recv()
+            gram[strip(0)] += gram_in[e]
+        lined = [
+            send(gram.at[p * cols + flipped(z, k)], gram_in.at[0, k],
+                 gram_s.at[0, k], gram_r.at[0, k], chip(0, k))
+            for k in range(1, cols)
+        ]
+        total = gram[me]
+        for k, made in enumerate(lined, 1):
+            made.wait_recv()
+            total += gram_in[0, k]
+        agop[me] = (total / point_count).astype(jnp.bfloat16)
+        back = [agop_copy(0, k) for k in range(1, cols)]
+        for made in back:
+            made.start()
+        for made in back:
+            made.wait_recv()
+        for e in range(1, planes):
+            back.append(copy(
+                agop.at[strip(0)], agop.at[strip(0)],
+                agop_s.at[e, 0], agop_r.at[e, 0], chip(e, 0),
+            ))
+            back[-1].start()
+        for made in back[cols - 1:]:
+            made.wait_recv()
+        sent.extend(back)
+    else:
         for d, k in peers:
-            gram_copy(d, k).wait_recv()
-            total += gram_in[d, k].astype(jnp.float32)
-        agop[place(me)] = (total / point_count).astype(jnp.bfloat16)
+            owning(flipped(p, d) * cols + flipped(z, k), gram_copy(d, k).start)
+
+        def reduce_own():
+            total = gram[place(me)]
+            for d, k in peers:
+                gram_copy(d, k).wait_recv()
+                total += gram_in[d, k]
+            agop[place(me)] = (total / point_count).astype(jnp.bfloat16)
+            for d, k in peers:
+                agop_copy(d, k).start()
+
+        owning(me, reduce_own)
         for d, k in peers:
-            agop_copy(d, k).start()
-
-    owning(me, reduce_own)
-    for d, k in peers:
-        owning(flipped(p, d) * cols + flipped(z, k), agop_copy(d, k).wait_recv)
+            owning(flipped(p, d) * cols + flipped(z, k), agop_copy(d, k).wait_recv)
 
     colored = lax.dot_general(
         rows[...].reshape(2 * count, width), agop[...].reshape(half, width), NT,
@@ -286,14 +321,15 @@
     line(lambda made: made.wait_send())
     for k in range(1, cols):
         onward(k, lambda made: made.wait_send())
-    for d, k in peers:
-        owning(flipped(p, d) * cols + flipped(z, k), gram_copy(d, k).wait_send)
-
-    def agop_sent():
+    if not every:
         for d, k in peers:
-            agop_copy(d, k).wait_send()
-
-    owning(me, agop_sent)
+            owning(flipped(p, d) * cols + flipped(z, k), gram_copy(d, k).wait_send)
+
+        def agop_sent():
+            for d, k in peers:
+                agop_copy(d, k).wait_send()
+
+        owning(me, agop_sent)
 
 
 def local(planes, cols, features, coefs):
@@ -324,8 +360,7 @@
             vmem((2 * count, width), f32),
             vmem((2 * count, width), bf16),
             vmem((owners, depth, width), f32),
-            vmem((owners, depth, width), bf16),
-            vmem((planes, cols, depth, width), bf16),
+            vmem((planes, cols, depth, width), f32),
             vmem((owners, depth, width), bf16),
             vmem((2, count, half), bf16),
             vmem((count, half), bf16),

time: 49.8 us -> 55.1 us (1.11)
  Pallas kernels: 46.1 us -> 51.5 us
    pallas_call x1, Pallas kernels: 46.1 us -> 51.5 us  [local(): pl.pallas_call(functools.partial(kernel, planes, cols, count * chips * 2)...]
where the time goes in v3:
time: 55.1 us; the launch traced here: 55 us
  Pallas kernels  51.5 us (93%)
  local copies, waits for them, and re-layouts  2.86 us (5%)
  between operations  0.65 us (1%)
    pallas_call x1, Pallas kernels, local(): pl.pallas_call(functools.partial(kernel, planes, cols, count * chips * 2)...  51.5 us
    unnamed x6, local copies, waits for them, and re-layouts  2.86 us

profile of v3, /device:TPU:0, one launch (start us, length us, event | category | flops | bytes accessed | tf_op | source)
XLA Modules:
  0.0 55.0 jit_solution(5808643560788052028)
XLA Ops:
  0.6 0.0 copy-start.1
  0.6 0.6 %copy-done.1 = bf16[128]{0:T(256)(128)(2,1)S(1)} copy-done((bf16[128]{0:T(256)(128)(2,1)S(1)}, bf16[128]{0:T(256)(128)(2,1)}, u32[]{:S(2)}) %copy-start.1) | copy-done | bytes 280
  1.3 0.0 copy-start
  1.3 0.9 %copy-done = bf16[128,512]{1,0:T(8,128)(2,1)S(1)} copy-done((bf16[128,512]{1,0:T(8,128)(2,1)S(1)}, bf16[128,512]{1,0:T(8,128)(2,1)}, u32[]{:S(2)}) %copy-start) | copy-done | bytes 131096
  2.2 51.5 %shard_map.41 = (bf16[128,512]{1,0:T(8,128)(2,1)S(1)}, bf16[128,512]{1,0:T(8,128)(2,1)S(1)}) custom-call(bf16[128,512]{1,0:T(8,128)(2,1)S(1)} %copy-done, bf16[1,128]{1,0:T(2,128)(2,1)S(1)} %bitcast.1), custom_call_target="tpu_custom_call" | custom-call | flops 1073741824 | bytes 393216 | tf_op jit(solution)/shard_map/pallas_call | solution.py:344
  53.7 0.7 %copy.6 = bf16[128,512]{1,0:T(8,128)(2,1)} copy(bf16[128,512]{1,0:T(8,128)(2,1)S(1)} %get-tuple-element.4) | data formatting | bytes 262144
  54.3 0.7 %copy.7 = bf16[128,512]{1,0:T(8,128)(2,1)} copy(bf16[128,512]{1,0:T(8,128)(2,1)S(1)} %get-tuple-element.5) | data formatting | bytes 262144
Async XLA Ops:
  0.6 0.7 %copy-start.1 = (bf16[128]{0:T(256)(128)(2,1)S(1)}, bf16[128]{0:T(256)(128)(2,1)}, u32[]{:S(2)}) copy-start(bf16[128]{0:T(256)(128)(2,1)} %param.3) | copy-start | bytes 772
  1.3 0.9 %copy-start = (bf16[128,512]{1,0:T(8,128)(2,1)S(1)}, bf16[128,512]{1,0:T(8,128)(2,1)}, u32[]{:S(2)}) copy-start(bf16[128,512]{1,0:T(8,128)(2,1)} %feat_hbm.1) | copy-start | bytes 393220
